TPU v7x, 128 devices: a whole 4x4x4 slice. The times are simulated.
128 devices in a mesh: dp: 32 (over z, x, core), section: 4 (over y).
Axes of the slice: x: 4, y: 4, z: 4, core: 2. Of those that a mesh axis runs over, the one named last changes fastest.
Arguments:
- tokens: bfloat16 [128, 197, 768], P(('dp', 'section')), may hold values from -6 to 6
- masked: int32 [128, 197], P(('dp', 'section')), may hold values from 0 to 1, as said below
- live_images: int32 [32], replicated, may hold values from 2 to 4, as said below
- mask_token: bfloat16 [768], replicated, may hold values from -5 to 5
- norm_gain: float32 [4, 768], P('section'), may hold values from 0.1 to 1.9
- norm_shift: float32 [4, 768], P('section'), may hold values from -3 to 3
- w_first: bfloat16 [4, 768, 3072], P('section')
- w_second: bfloat16 [2, 3072, 768], replicated, may hold values from -0.109375 to 0.109375
- layer_scale: float32 [4, 768], P('section'), may hold values from 0.5 to 2
- rel_table: float32 [2, 732, 12], replicated, may hold values from -4 to 4
- cotangent: bfloat16 [128, 197, 768], P(('dp', 'section')), may hold values from -6 to 6
Outputs:
- block_out: bfloat16 [128, 197, 768], P(('dp', 'section'))
- tokens_grad: bfloat16 [128, 197, 768], P(('dp', 'section'))
- first_grad: float32 [4, 768, 3072], P('section')
- second_grad: float32 [2, 3072, 768], P(None, ('dp', 'section'))
- gain_grad: float32 [4, 768], P('section')
- shift_grad: float32 [4, 768], P('section')
- scale_grad: float32 [4, 768], P('section')
- table_grad: float32 [2, 732, 12], replicated
- mask_grad: float32 [768], replicated
- rms_out: float32 [4, 2], replicated
Inputs may be any that keep to these rules, and one draw needn't show every extreme that they name: The class token (position 0) of every image is never masked. `live_images`: images in use of the 4 slots of one index of dp; the unused slots are the last ones of that index; some index is full.
All inputs are finite; a program needn't handle non-finite values.
Results may differ from a plain program's by a relative error of at most 0.025.
Values may be sent and summed in bfloat16 or wider, within the bound.
A program may use at most 512 MiB of HBM per device.

v0:
```python
import functools
import math

import jax
import jax.numpy as jnp
from jax import lax
from jax.experimental import pallas as pl
from jax.experimental.pallas import tpu as pltpu
from jax.sharding import PartitionSpec as P

SEQ, ROWS, KEYS = 197, 208, 256
D, FF, HEADS, GRID = 768, 3072, 12, 14
SPAN = 2 * GRID - 1
EPSILON = 1e-06
INV_ROOT = 0.125
INV_ROOT_TWO_PI = 0.3989422804014327
F32, BF16 = jnp.float32, jnp.bfloat16
HALF = (3, 4, 4, 4, 16, 384)


def mm(a, b):
    return lax.dot_general(a, b, (((1,), (0,)), ((), ())), preferred_element_type=F32)


def mm_nt(a, b):
    return lax.dot_general(a, b, (((1,), (1,)), ((), ())), preferred_element_type=F32)


def mm_tn(a, b):
    return lax.dot_general(a, b, (((0,), (0,)), ((), ())), preferred_element_type=F32)


def lanes(start, size):
    return pl.ds(pl.multiple_of(start, 128), size)


def patch_offsets(token):
    patch = token - 1
    return patch + (SPAN - GRID) * ((patch * 4682) >> 16)


def ones(condition):
    return jnp.where(condition, 1.0, 0.0).astype(BF16)


def centre(h):
    average = jnp.mean(h, axis=-1, keepdims=True)
    centred = h - average
    inv_std = lax.rsqrt(jnp.mean(centred * centred, axis=-1, keepdims=True) + EPSILON)
    return centred * inv_std, inv_std


def gelu_pair(u):
    size = jnp.abs(u)
    t = 1.0 / (1.0 + 0.23164189 * size)
    bell = jnp.exp(-0.5 * u * u)
    poly = t * (
        0.127414796
        + t * (-0.142248368 + t * (0.7107068705 + t * (-0.7265760135 + t * 0.5307027145)))
    )
    tail = poly * bell
    phi = jnp.where(u >= 0.0, 1.0 - tail, tail)
    return u * phi, phi + u * bell * INV_ROOT_TWO_PI


def half_mask(rows, parity):
    lane = lax.broadcasted_iota(jnp.int32, (rows, 128), 1)
    return (lane < 64) if parity == 0 else (lane >= 64)


def keep_half(block, parity):
    return jnp.where(half_mask(block.shape[0], parity), block, jnp.zeros_like(block))


class Body:
    def __init__(self, **refs):
        self.__dict__.update(refs)

    def make_selectors(self):
        row = lax.broadcasted_iota(jnp.int32, (384, KEYS), 0)
        token = lax.broadcasted_iota(jnp.int32, (384, KEYS), 1)
        self.select_forward[...] = ones((row == patch_offsets(token)) & (token > 0) & (token < SEQ))
        row = lax.broadcasted_iota(jnp.int32, (16 * GRID, ROWS), 0)
        token = lax.broadcasted_iota(jnp.int32, (16 * GRID, ROWS), 1)
        patch = token - 1
        y = (patch * 4682) >> 16
        wanted = jnp.where(token == 0, GRID, (patch - GRID * y) * 16 + y)
        self.by_x[...] = ones((row == wanted) & (token < SEQ))

    def read_tables(self, tables):
        shape = (tables.shape[2], 896)
        entry = lax.broadcasted_iota(jnp.int32, shape, 0)
        lane = lax.broadcasted_iota(jnp.int32, shape, 1)
        source = jnp.where(lane < 768, SPAN * SPAN - 1 - lane, lane + (SPAN * SPAN - 768))
        select = ones(entry == source)
        for layer in range(2):
            self.table[layer * HEADS : (layer + 1) * HEADS, :] = mm(tables[:, layer, :].astype(BF16), select)

    def expand_bias(self, layer, lo, hi):
        def head(index, _):
            entries = self.table[pl.ds(layer * HEADS + index, 1), :]
            base = jnp.broadcast_to(entries[:, :768], (16, 768))
            base = pltpu.roll(base, 404, 1, stride=1, stride_axis=0)
            for yi in range(GRID):
                turned = pltpu.roll(base, SPAN * yi, 1) if yi else base
                for t in range(3):
                    self.sums[t, 1 + GRID * yi : 1 + GRID * (yi + 1), :] = turned[:GRID, 128 * t : 128 * t + 128]
            spread = jnp.concatenate([self.sums[0], self.sums[1], self.sums[2]], axis=1)
            grid = mm(spread.astype(BF16), self.select_forward[...])
            row = lax.broadcasted_iota(jnp.int32, (ROWS, KEYS), 0)
            column = lax.broadcasted_iota(jnp.int32, (ROWS, KEYS), 1)
            corner = entries[:, 768:]
            grid = jnp.where(row == 0, corner[:, 0:1], grid)
            grid = jnp.where(column == 0, corner[:, 1:2], grid)
            grid = jnp.where((row == 0) & (column == 0), corner[:, 2:3], grid)
            self.bias[layer, index] = jnp.where(column >= SEQ, -1e30, grid).astype(BF16)
            return 0

        lax.fori_loop(lo, hi, head, 0)

    def normed(self, s):
        scaled, _ = centre(self.h[s].astype(F32))
        gain = self.vecs[s, 0:1, :]
        shift = self.vecs[s, 1:2, :]
        self.n[0] = (scaled * gain + shift).astype(BF16)

    def note(self, row, value):
        self.small[pl.ds(row, 1), :] = value

    def finish(self, s, left, right):
        real = (lax.broadcasted_iota(jnp.int32, (ROWS, 1), 0) < SEQ).astype(F32) * self.valid

        projected = mm(left[...], right)
        branch = self.vecs[s, 2:3, :] * projected
        result = self.h[s].astype(F32) + branch
        self.p[s] = projected.astype(BF16)
        self.note(2 * s, jnp.sum(branch * branch * real, axis=0, keepdims=True))
        self.note(2 * s + 1, jnp.sum(result * result * real, axis=0, keepdims=True))

        @pl.when(s < 3)
        def _():
            self.h[s + 1] = result.astype(BF16)

        @pl.when(s == 3)
        def _():
            self.block_out[0] = (result[:SEQ] * self.valid).astype(BF16)

    def attend_forward(self, layer):
        s = 2 * layer
        self.normed(s)

        def project(j, _):
            columns = lanes(j * 1152, 1152)
            weights = self.w[s, :, :, :, columns].reshape(D, 1152)
            self.qkv[layer, :ROWS, columns] = mm(self.n[0], weights).astype(BF16)
            return 0

        lax.fori_loop(0, 2, project, 0)
        self.qkv[layer, ROWS:, :] = jnp.zeros((KEYS - ROWS, 2304), BF16)

        def pair(j):
            q = self.qkv[layer, :ROWS, lanes(j * 128, 128)]
            k = self.qkv[layer, :, lanes(768 + j * 128, 128)]
            v = self.qkv[layer, :, lanes(1536 + j * 128, 128)]
            mixed = jnp.zeros((ROWS, 128), F32)
            for parity in range(2):
                scores = mm_nt(keep_half(q, parity), k) * INV_ROOT + self.bias[layer, 2 * j + parity].astype(F32)
                peak = jnp.max(scores, axis=-1, keepdims=True)
                exps = jnp.exp(scores - peak)
                total = jnp.sum(exps, axis=-1, keepdims=True)
                probs = (exps * (1.0 / total)).astype(BF16)
                self.probs[layer, 2 * j + parity, :ROWS] = probs
                mixed = mixed + mm(probs, keep_half(v, parity))
            self.o[layer, :, lanes(j * 128, 128)] = mixed.astype(BF16)

        def pairs(i, _):
            for j in range(3):
                pair(3 * i + j)
            return 0

        lax.fori_loop(0, 2, pairs, 0)
        self.finish(s, self.o.at[layer], self.w[s, :, :, :, 2304:].reshape(D, D))

    def dense_forward(self, layer):
        s = 2 * layer + 1
        self.normed(s)

        def up(j, _):
            columns = lanes(j * 1024, 1024)
            u = mm(self.n[0], self.w[s, :, :, :, columns].reshape(D, 1024))
            act, slope = gelu_pair(u)
            self.a[layer, :, columns] = act.astype(BF16)
            self.slope[layer, :, columns] = slope.astype(BF16)
            return 0

        lax.fori_loop(0, 3, up, 0)
        self.finish(s, self.a.at[layer], self.w2[...])

    def enter(self, layer, dense):
        s = 2 * layer + dense
        g = self.g[...].astype(F32)
        row = 8 + 3 * s
        self.note(row, jnp.sum(g * self.p[s].astype(F32), axis=0, keepdims=True))
        dp = (g * self.vecs[s, 2:3, :]).astype(BF16)
        self.dp[...] = dp
        self.normed(s)
        if not dense:
            self.n[1] = self.o[layer]
            self.du[:, 2304:] = dp

    def leave(self, layer, dense):
        s = 2 * layer + dense
        width = FF if dense else 2304
        dn = mm_nt(self.du[:, :width], self.w[s, :, :, :, :width].reshape(D, width))
        scaled, inv_std = centre(self.h[s].astype(F32))
        row = 8 + 3 * s
        self.note(row + 1, jnp.sum(dn * scaled, axis=0, keepdims=True))
        self.note(row + 2, jnp.sum(dn, axis=0, keepdims=True))
        e = dn * self.vecs[s, 0:1, :]
        mean_e = jnp.mean(e, axis=-1, keepdims=True)
        mean_ex = jnp.mean(e * scaled, axis=-1, keepdims=True)
        g = self.g[...].astype(F32) + inv_std * (e - mean_e - scaled * mean_ex)
        self.g[...] = g.astype(BF16)

    def put(self, t, mine, route, a1, a2, a3, piece):
        if mine:
            pair = self.pair.at[t.slot, route, a1, a2, a3]
            pair[...] = (piece + pair[...].astype(F32)).astype(BF16)
        else:
            self.stage[t.slot, route, a1, a2, a3] = piece.astype(BF16)

    def first_half(self, t, mine):
        half = self.core if mine else 1 - self.core

        def block(i, _):
            if mine:
                self.reduce.swapped(t, i)
            j = half * 2 + i
            left = jnp.where(j == 3, 1, 0) if t.which == 2 else 0
            grad = mm_tn(self.n[left], self.du[:, lanes(j * 768, 768)])
            for side in range(2):
                for rb in range(16):
                    for route in range(3):
                        top = rb * 48 + route * 16
                        self.put(
                            t, mine, route, rb // 4, rb % 4, 2 * i + side,
                            grad[top : top + 16, 384 * side : 384 * side + 384],
                        )
            if not mine:
                self.reduce.swap(t, i)
            return 0

        lax.fori_loop(0, 2, block, 0)

    def second_half(self, t, mine):
        half = self.core if mine else 1 - self.core

        def block(i, _):
            if mine:
                self.reduce.swapped(t, i)
            grad = mm_tn(self.a[t.layer, :, lanes(i * 1536, 1536)], self.dp[:, lanes(half * 384, 384)])
            for z_low in range(2):
                z = 2 * i + z_low
                for x in range(4):
                    for y in range(4):
                        top = (z_low * 4 + x) * 192 + y * 24
                        part = jnp.concatenate([grad[top : top + 24], grad[top + 96 : top + 120]], axis=0)
                        self.put(t, mine, 0, x, y, z, part[0:16])
                        self.put(t, mine, 1, y, z, x, part[16:32])
                        self.put(t, mine, 2, z, x, y, part[32:48])
            if not mine:
                self.reduce.swap(t, i)
            return 0

        lax.fori_loop(0, 2, block, 0)

    def down(self, layer):
        def block(j, _):
            columns = lanes(j * 1536, 1536)
            rows = pl.ds(pl.multiple_of(j * 1536, 256), 1536)
            da = mm_nt(self.dp[...], self.w2[rows, :])
            self.du[:, columns] = (da * self.slope[layer, :, columns].astype(F32)).astype(BF16)
            return 0

        lax.fori_loop(0, 2, block, 0)

    def back_out(self, layer):
        weights = self.w[2 * layer, :, :, :, 2304:].reshape(D, D)
        self.dp[...] = mm_nt(self.du[:, 2304:], weights).astype(BF16)

    def pairs(self, layer, third):
        def pair(j):
            q = self.qkv[layer, :ROWS, lanes(j * 128, 128)]
            k = self.qkv[layer, :, lanes(768 + j * 128, 128)]
            v = self.qkv[layer, :, lanes(1536 + j * 128, 128)]
            do = self.dp[:, lanes(j * 128, 128)]
            dq = jnp.zeros((ROWS, 128), F32)
            dk = jnp.zeros((KEYS, 128), F32)
            dv = jnp.zeros((KEYS, 128), F32)
            for parity in range(2):
                do_half = keep_half(do, parity)
                probs = self.probs[layer, 2 * j + parity, :ROWS]
                wide = probs.astype(F32)
                d_probs = mm_nt(do_half, v)
                inner = jnp.sum(d_probs * wide, axis=-1, keepdims=True)
                d_scores = (wide * (d_probs - inner)).astype(BF16)
                dv = dv + mm_tn(probs, do_half)
                dq = dq + mm(d_scores, keep_half(k, parity))
                dk = dk + mm_tn(d_scores, keep_half(q, parity))
                self.probs[layer, 2 * j + parity] = mm(self.by_x[...], d_scores).astype(BF16)
            self.du[:, lanes(j * 128, 128)] = (dq * INV_ROOT).astype(BF16)
            self.du[:, lanes(768 + j * 128, 128)] = (dk[:ROWS] * INV_ROOT).astype(BF16)
            self.du[:, lanes(1536 + j * 128, 128)] = dv[:ROWS].astype(BF16)

        def trio(i, _):
            for j in range(3):
                pair(3 * i + j)
            return 0

        lax.fori_loop(third, third + 1, trio, 0)

    def fold_bias(self, layer):
        shape = (KEYS, 384)
        token = lax.broadcasted_iota(jnp.int32, shape, 0)
        lane = lax.broadcasted_iota(jnp.int32, shape, 1)
        target = jnp.where(token >= SEQ, -1000, (SPAN + 1) * (GRID - 1) - patch_offsets(token))
        self.sums[...] = jnp.zeros((3, ROWS, 128), F32)

        def two(i, _):
            lefts, rights = [], []
            for odd in range(2):
                x = 2 * i + odd
                rows = pl.ds(pl.multiple_of(16 * x, 16), 16)
                lefts.append(self.probs[layer, :, rows, :].reshape(192, KEYS))
                here = jnp.where(token == 0, 383, target + x)
                rights.append(ones(lane == here))
            more = mm(jnp.concatenate(lefts, axis=1), jnp.concatenate(rights, axis=0))
            for t in range(3):
                self.sums[t, :192] += more[:, 128 * t : 128 * t + 128]
            return 0

        lax.fori_loop(0, GRID // 2, two, 0)
        last = lax.broadcasted_iota(jnp.int32, (HEADS, 384), 1) == 383
        total = jnp.zeros((HEADS, D), F32)
        side = jnp.zeros((HEADS, 1), F32)
        for y in range(GRID + 1):
            rows = jnp.concatenate([self.sums[t, pl.ds(y, HEADS, stride=16), :] for t in range(3)], axis=1)
            plain = jnp.where(last, 0.0, rows)
            if y < GRID:
                side = side + jnp.sum(rows - plain, axis=1, keepdims=True)
                wide = jnp.concatenate([plain, jnp.zeros((HEADS, 384), F32)], axis=1)
                total = total + (pltpu.roll(wide, SPAN * y, 1) if y else wide)
            else:
                top = jnp.sum(plain, axis=1, keepdims=True)
                corner = jnp.sum(rows - plain, axis=1, keepdims=True)
        entry = lax.broadcasted_iota(jnp.int32, (HEADS, D), 1)
        total = jnp.where(entry == 729, top, total)
        total = jnp.where(entry == 730, side, total)
        total = jnp.where(entry == 731, corner, total)
        for head in range(HEADS):
            self.note(24 + layer * HEADS + head, total[head : head + 1])


MESH = pl.DeviceIdType.MESH
AXES = ("x", "y", "z")
ROUTES = (("x", "y", "z"), ("y", "z", "x"), ("z", "x", "y"))


class Place:
    def __init__(self):
        dp = lax.axis_index("dp")
        self.at = {"z": dp // 8, "x": (dp // 2) % 4, "c": dp % 2, "y": lax.axis_index("section")}

    def go(self, axis, step):
        at = dict(self.at)
        at[axis] = (at[axis] + step) % (2 if axis == "c" else 4)
        return ((at["z"] * 4 + at["x"]) * 2 + at["c"], at["y"])

    def index(self, axis, step=0):
        return (self.at[axis] + step) % 4


def meet(place):
    barrier = pltpu.get_barrier_semaphore()
    count = 0
    for axis in AXES:
        for step in (1, 2, 3):
            pl.semaphore_signal(barrier, inc=1, device_id=place.go(axis, step), device_id_type=MESH)
            count += 1
    pl.semaphore_signal(barrier, inc=1, device_id=place.go("c", 1), device_id_type=MESH)
    pl.semaphore_wait(barrier, count + 1)


class Tensor:
    def __init__(self, turn, which):
        self.number, self.slot = 3 * turn + which, (turn + which) % 2
        self.layer, self.which = 1 - turn, which
        self.second = which == 0
        self.section = 2 * self.layer + (which == 1)


class Reduce:
    def __init__(self, place, **refs):
        self.place = place
        self.__dict__.update(refs)

    def link(self, t, number, src, dst, device):
        return pltpu.make_async_remote_copy(
            src_ref=src, dst_ref=dst, send_sem=self.sems.at[0, t.number, number],
            recv_sem=self.sems.at[1, t.number, number], device_id=device, device_id_type=MESH,
        )

    def ring(self, name, t, r):
        place, axis = self.place, ROUTES[r][0]
        own, far = self.pair.at[t.slot, r], self.far.at[t.slot, r]
        across, ahead, behind = place.index(axis, 2), place.index(axis, 1), place.index(axis, 3)
        source, number, step = {
            "fa": lambda: (own.at[across, 0:2], 0, 1),
            "fb": lambda: (own.at[across, 2:4], 1, 3),
            "db": lambda: (own.at[ahead, 2:4], 2, 1),
            "da": lambda: (own.at[behind, 0:2], 3, 3),
            "ma": lambda: (far.at[0], 4, 1),
            "mb": lambda: (far.at[1], 5, 3),
        }[name]()
        return self.link(t, 6 + 6 * r + number, source, far.at[number], place.go(axis, step))

    def line_copy(self, t, r, step):
        axis = ROUTES[r][1]
        source = self.line.at[t.slot, r, self.place.index(axis, step)]
        return self.link(t, 23 + 3 * r + step, source, self.line_in.at[t.slot, r, step - 1], self.place.go(axis, step))

    def spot_copy(self, t, r, step):
        axis = ROUTES[r][2]
        source = self.spot.at[t.slot, r, self.place.index(axis, step)]
        return self.link(t, 32 + 3 * r + step, source, self.spot_in.at[t.number, r, step - 1], self.place.go(axis, step))

    def rows_copy(self, t):
        source = self.rows.at[t.layer, 1 - self.place.at["c"]]
        return self.link(t, 42, source, self.rows_in.at[t.layer], self.place.go("c", 1))

    def part(self, buffer, t, i):
        pair = pl.ds(2 * i, 2)
        if not t.second:
            return [(3 * i, buffer.at[t.slot, :, :, :, pair])]
        return [
            (3 * i, buffer.at[t.slot, 0, :, :, pair]),
            (3 * i + 1, buffer.at[t.slot, 1, :, pair]),
            (3 * i + 2, buffer.at[t.slot, 2, pair]),
        ]

    def across(self, t, i):
        for (number, source), (_, target) in zip(self.part(self.stage, t, i), self.part(self.pair, t, i)):
            yield self.link(t, number, source, target, self.place.go("c", 1))

    def prepare(self, t, before):
        for i in range(2):
            for copy in self.across(before, i):
                copy.wait_send()
        pl.semaphore_wait(self.pair_credit, 1)

    def swap(self, t, i):
        for copy in self.across(t, i):
            copy.start()

    def swapped(self, t, i):
        for copy in self.across(t, i):
            copy.wait_recv()

    def first(self, t):
        for r in range(3):
            @pl.when(t.number >= 2)
            def _():
                pl.semaphore_wait(self.far_credit.at[r, 0], 1)
                pl.semaphore_wait(self.far_credit.at[r, 1], 1)

            for name in ("fa", "fb", "db", "da"):
                self.ring(name, t, r).start()

    def merge(self, t):
        place = self.place
        for r, (axis, _, _) in enumerate(ROUTES):
            own, far = self.pair.at[t.slot, r], self.far.at[t.slot, r]
            ahead, behind = place.index(axis, 1), place.index(axis, 3)
            self.ring("fa", t, r).wait_recv()
            far[0] = (far[0].astype(F32) + own[ahead, 0:2].astype(F32)).astype(BF16)
            self.ring("ma", t, r).start()
            self.ring("fb", t, r).wait_recv()
            far[1] = (far[1].astype(F32) + own[behind, 2:4].astype(F32)).astype(BF16)
            self.ring("mb", t, r).start()

    def second(self, t):
        place = self.place
        for r in range(3):
            for name in ("db", "da", "ma", "mb"):
                self.ring(name, t, r).wait_recv()
        for r, (axis, nxt, _) in enumerate(ROUTES):
            own, far = self.pair.at[t.slot, r], self.far.at[t.slot, r]
            me = place.index(axis)
            low = own[me, 0:2].astype(F32) + far[4].astype(F32) + far[3].astype(F32)
            high = own[me, 2:4].astype(F32) + far[2].astype(F32) + far[5].astype(F32)
            line = self.line.at[t.slot, r]
            line[0:2] = low.astype(BF16)
            line[2:4] = high.astype(BF16)
            for step in (1, 2, 3):
                self.line_copy(t, r, step).start()
        for r in range(3):
            for name in ("fa", "fb", "db", "da", "ma", "mb"):
                self.ring(name, t, r).wait_send()

        @pl.when(t.number + 2 < 6)
        def _():
            pl.semaphore_signal(self.pair_credit, inc=1, device_id=place.go("c", 1), device_id_type=MESH)
            for r, (axis, _, _) in enumerate(ROUTES):
                pl.semaphore_signal(self.far_credit.at[r, 0], inc=1, device_id=place.go(axis, 1), device_id_type=MESH)
                pl.semaphore_signal(self.far_credit.at[r, 1], inc=1, device_id=place.go(axis, 3), device_id_type=MESH)

    def third(self, t):
        for r, (_, axis, _) in enumerate(ROUTES):
            total = self.line[t.slot, r, self.place.index(axis)].astype(F32)
            for step in (1, 2, 3):
                self.line_copy(t, r, step).wait_recv()
                total = total + self.line_in[t.slot, r, step - 1].astype(F32)
            self.spot[t.slot, r] = total.astype(BF16)
            for step in (1, 2, 3):
                self.spot_copy(t, r, step).start()
        for r in range(3):
            for step in (1, 2, 3):
                self.line_copy(t, r, step).wait_send()

    def close(self, t):
        for r, (_, _, axis) in enumerate(ROUTES):
            total = self.spot[t.slot, r, self.place.index(axis)].astype(F32)
            for step in (1, 2, 3):
                self.spot_copy(t, r, step).wait_recv()
                total = total + self.spot_in[t.number, r, step - 1].astype(F32)
            if not t.second:
                self.first_out[t.section, 0, 0, r] = total.astype(BF16)
            elif r == 0:
                self.rows[t.layer, 0, 0:16] = total
            elif r == 1:
                self.rows[t.layer, 0, 16:24] = total[0:8]
                self.rows[t.layer, 1, 0:8] = total[8:16]
            else:
                self.rows[t.layer, 1, 8:24] = total
        for r in range(3):
            for step in (1, 2, 3):
                self.spot_copy(t, r, step).wait_send()
        if t.second:
            self.rows_copy(t).start()

    def finish(self):
        me = self.place.at["c"]
        for turn in range(2):
            t = Tensor(turn, 0)
            self.rows_copy(t).wait()
            self.second_out[t.layer, :, lanes(me * 384, 384)] = self.rows[t.layer, me]
            self.second_out[t.layer, :, lanes((1 - me) * 384, 384)] = self.rows_in[t.layer]
        for which in (1, 2):
            for i in range(2):
                for copy in self.across(Tensor(1, which), i):
                    copy.wait_send()


class Totals:
    def __init__(self, place, part, bufs, sems):
        self.place, self.part, self.bufs, self.sems = place, part, bufs, sems
        self.copies = []

    def send(self, src, dst, number, device):
        copy = pltpu.make_async_remote_copy(
            src_ref=src, dst_ref=dst, send_sem=self.sems.at[0, number], recv_sem=self.sems.at[1, number],
            device_id=device, device_id_type=MESH,
        )
        copy.start()
        self.copies.append(copy)
        return copy

    @staticmethod
    def half(core):
        return pl.ds(pl.multiple_of(core * 24, 8), 24)

    def start(self, small):
        me = self.place.at["c"]
        self.small = small
        self.now = [self.send(small.at[self.half(1 - me)], self.bufs.at[12], 0, self.place.go("c", 1))]

    def step(self, number):
        place, me = self.place, self.place.at["c"]
        for copy in self.now:
            copy.wait_recv()
        if number == 0:
            self.part[...] = self.small[self.half(me), :] + self.bufs[12]
        else:
            axis = AXES[number - 1]
            self.bufs[4 * number - 4 + place.at[axis]] = self.part[...]
            self.part[...] = (
                (self.bufs[4 * number - 4] + self.bufs[4 * number - 3])
                + (self.bufs[4 * number - 2] + self.bufs[4 * number - 1])
            )
        if number < 3:
            axis = AXES[number]
            self.now = [
                self.send(self.part, self.bufs.at[4 * number + place.at[axis]], 1 + 3 * number + step - 1, place.go(axis, step))
                for step in (1, 2, 3)
            ]
            for copy in self.now:
                copy.wait_send()
        else:
            self.now = [self.send(self.part, self.bufs.at[13], 10, place.go("c", 1))]

    def close(self, out):
        me = self.place.at["c"]
        for copy in self.now:
            copy.wait_recv()
        out[self.half(me), :] = self.part[...]
        out[self.half(1 - me), :] = self.bufs[13]
        self.copies[0].wait_send()
        self.copies[-1].wait_send()


class Spread:
    def __init__(self, place, sems):
        self.place, self.sems = place, sems
        self.sent = []

    def make(self, number, src, dst, device):
        return pltpu.make_async_remote_copy(
            src_ref=src, dst_ref=dst, send_sem=self.sems.at[0, number], recv_sem=self.sems.at[1, number],
            device_id=device, device_id_type=MESH,
        )

    def send(self, number, src, dst, device):
        copy = self.make(number, src, dst, device)
        copy.start()
        self.sent.append(copy)

    def wait(self, number, ref):
        pltpu.make_async_remote_copy(
            src_ref=ref, dst_ref=ref, send_sem=self.sems.at[0, number], recv_sem=self.sems.at[1, number],
            device_id=self.place.go("c", 1), device_id_type=MESH,
        ).wait_recv()

    def drain(self):
        for copy in self.sent:
            copy.wait_send()


GATHER_MESSAGES = 99


class Gather(Spread):
    def __init__(self, place, full, sems):
        super().__init__(place, sems)
        self.full = full
        y = place.at["y"]
        self.first = {"x": 3, "z": 1}
        self.second = {"x": jnp.where(y == 3, 1, 2), "z": jnp.where(y == 1, 3, 2)}
        self.third = {"x": jnp.where(y == 3, 2, 1), "z": jnp.where(y == 1, 2, 3)}

    def rows(self, route, step, sub=None, core=None):
        core = self.place.at["c"] if core is None else core
        block = (0 if route == "x" else 8) + self.place.index(route, step) * 2 + core
        return (block // 4, block % 4, slice(None) if sub is None else slice(16 * sub, 16 * sub + 16))

    def ref(self, rel, route, step, sub=None):
        return self.full.at[(self.place.index("y", rel),) + self.rows(route, step, sub)]

    @staticmethod
    def along_y(rel, route, sub):
        return 3 * (2 * (rel - 1) + (route == "z")) + sub

    @staticmethod
    def in_plane(rel, route, kind, sub):
        return 18 + 9 * (2 * (rel - 1) + (route == "z")) + 3 * kind + sub

    @staticmethod
    def across(rel, route, step):
        return 72 + 4 * (2 * (rel - 1) + (route == "z")) + step

    def load(self, source, sems):
        at = self.place.at
        mine, rest = [], []
        for half, route in enumerate(("x", "z")):
            for block in range(8):
                number = 8 * half + (at[route] * 2 + at["c"] + block) % 8
                rows = pl.ds(pl.multiple_of(number * 48, 16), 48)
                copy = pltpu.make_async_copy(
                    source.at[rows], self.full.at[at["y"], number // 4, number % 4], sems.at[half, block]
                )
                (rest if block else mine).append(copy)
        for copy in mine + rest:
            copy.start()
        for copy in mine:
            copy.wait()
        return rest

    def own(self, up, down):
        copies = []
        for sub in range(3):
            for route, step in ((up, 1), (down, 3)):
                mine = self.ref(0, route, 0, sub)
                copies.append(self.make(self.along_y(4 - step, route, sub), mine, mine, self.place.go("y", step)))
        self.sent += copies
        return copies

    def arrive(self, rels):
        for sub in range(3):
            for route, rel in rels.items():
                piece = self.ref(rel, route, 0, sub)
                self.wait(self.along_y(rel, route, sub), piece)
                if rels is self.first:
                    self.send(self.along_y(2, route, sub), piece, piece, self.place.go("y", 4 - rel))
                for kind, step in ((0, 1), (1, 3)):
                    self.send(self.in_plane(rel, route, kind, sub), piece, piece, self.place.go(route, step))
        for route, rel in rels.items():
            piece = self.ref(rel, route, 0)
            self.send(self.across(rel, route, 0), piece, piece, self.place.go("c", 1))

    def turn(self, rels):
        place = self.place
        clockwise = 1 - 2 * place.at["c"]
        for sub, way in ((0, 1), (1, clockwise), (2, -1)):
            for route, rel in rels.items():
                for kind, step in ((0, 3), (1, 1)):
                    self.wait(self.in_plane(rel, route, kind, sub), self.ref(rel, route, step, sub))
                piece = self.ref(rel, route, 4 - way, sub)
                self.send(self.in_plane(rel, route, 2, sub), piece, piece, place.go(route, 4 + way))
        for route, rel in rels.items():
            for step in (3, 1):
                piece = self.ref(rel, route, step)
                self.send(self.across(rel, route, step), piece, piece, place.go("c", 1))

    def end(self, rels):
        for route, rel in rels.items():
            for sub in range(3):
                self.wait(self.in_plane(rel, route, 2, sub), self.ref(rel, route, 2, sub))
            piece = self.ref(rel, route, 2)
            self.send(self.across(rel, route, 2), piece, piece, self.place.go("c", 1))

    def ending(self, rels):
        waits, copies = [], []
        for route, rel in rels.items():
            for sub in range(3):
                ref = self.ref(rel, route, 2, sub)
                waits.append(self.make(self.in_plane(rel, route, 2, sub), ref, ref, self.place.go("c", 1)))
            piece = self.ref(rel, route, 2)
            copies.append(self.make(self.across(rel, route, 2), piece, piece, self.place.go("c", 1)))
        self.sent += copies
        return waits, copies

    def settle(self, section):
        rel = (section - self.place.at["y"] + 4) % 4
        other = 1 - self.place.at["c"]

        def run():
            for route in ("x", "z"):
                for step in range(4):
                    self.wait(self.across(rel, route, step), self.full.at[(section,) + self.rows(route, step, core=other)])

        pl.when(rel > 0)(run)


def layers_kernel(
    tokens, masked, cotangent, live, mask_token, norm_gain, norm_shift, layer_scale, w_own, w2_hbm,
    tables,
    block_out, tokens_grad, first_grad, second_out, totals,
    w, w2, h, qkv, probs, o, a, slope, p, n, bias, table, select_f, by_x, fold_sums, du, dp, g, vec, vecs, small,
    stage, pair, far, line, line_in, spot, spot_in, rows, rows_in, part, bufs, first_out,
    load_sems, w2_sems, gather_sems, sems, small_sems, share_sems, share_out_sems, pair_credit, far_credit,
):
    place = Place()
    vec[0:1] = norm_gain[...]
    vec[1:2] = norm_shift[...]
    vec[2:3] = layer_scale[...]
    vec[3:8] = jnp.zeros((5, D), F32)
    meet(place)
    y = place.at["y"]
    gather = Gather(place, w, gather_sems)
    own_rest = gather.load(w_own.at[0], load_sems)
    for copy in gather.own("x", "z"):
        copy.start()
    own_later = gather.own("z", "x")

    @pl.when(y == 0)
    def _():
        for copy in own_later:
            copy.start()

    def second_weights(layer):
        copies = []
        for block in range(8):
            rows = pl.ds(block * 384, 384)
            copies.append(pltpu.make_async_copy(w2_hbm.at[layer, rows], w2.at[rows], w2_sems.at[block]))
        return copies

    def load_second(layer):
        for copy in second_weights(layer):
            copy.start()

    def loaded_second(layer):
        for copy in second_weights(layer):
            copy.wait()

    def loaded(copies):
        for copy in copies:
            copy.wait()

    load_second(0)
    vecs[y] = vec[...]
    for step in (1, 2, 3):
        gather.send(95 + step, vec, vecs.at[y], place.go("y", step))
    valid = jnp.where(y < live[lax.axis_index("dp")], 1.0, 0.0)
    body = Body(
        valid=valid, core=place.at["c"], vecs=vecs, table=table,
        select_forward=select_f, by_x=by_x, block_out=block_out, small=small,
        w=w, w2=w2, h=h, qkv=qkv, probs=probs, o=o, a=a, slope=slope, p=p, n=n, bias=bias,
        sums=fold_sums, du=du, dp=dp, g=g, stage=stage, pair=pair,
    )
    reduce = Reduce(
        place, stage=stage, pair=pair, far=far, line=line, line_in=line_in, spot=spot, spot_in=spot_in,
        rows=rows, rows_in=rows_in, first_out=first_out, second_out=second_out, sems=sems,
        pair_credit=pair_credit, far_credit=far_credit,
    )
    body.reduce = reduce
    sums = Totals(place, part, bufs, small_sems)

    gather.arrive(gather.first)

    @pl.when(y != 0)
    def _():
        for copy in own_later:
            copy.start()

    fold_sums[...] = jnp.zeros_like(fold_sums)
    square = (ROWS, KEYS)
    diagonal = lax.broadcasted_iota(jnp.int32, square, 0) == lax.broadcasted_iota(jnp.int32, square, 1)
    flags = jnp.concatenate([masked[...].astype(F32), jnp.zeros((1, KEYS - SEQ), F32)], axis=1)
    here = jnp.sum(jnp.where(diagonal, flags, 0.0), axis=1, keepdims=True)
    h[0, 192:] = jnp.zeros((16, D), BF16)
    start = tokens[0].astype(F32)
    h[0, :SEQ] = (start + here[:SEQ] * (mask_token[...].astype(F32).reshape(1, D) - start)).astype(BF16)
    g[192:] = jnp.zeros((16, D), BF16)
    g[:SEQ] = (cotangent[0].astype(F32) * valid).astype(BF16)
    body.make_selectors()
    body.read_tables(tables)
    body.expand_bias(0, 0, 6)
    gather.arrive(gather.second)
    body.expand_bias(0, 6, 12)
    gather.turn(gather.first)
    body.expand_bias(1, 0, 6)
    gather.arrive(gather.third)
    gather.turn(gather.second)
    body.expand_bias(1, 6, 12)
    gather.end(gather.first)
    gather.end(gather.second)
    for step in (1, 2, 3):
        gather.wait(95 + step, vecs.at[place.index("y", 4 - step)])
    loaded(own_rest)
    gather.turn(gather.third)
    last_waits, last_copies = gather.ending(gather.third)

    def forward_layer(layer, _):
        gather.settle(2 * layer)
        body.attend_forward(layer)

        @pl.when(layer == 0)
        def _():
            for copy in last_waits:
                copy.wait_recv()
            for copy in last_copies:
                copy.start()

        gather.settle(2 * layer + 1)
        loaded_second(layer)
        body.dense_forward(layer)

        @pl.when(layer == 0)
        def _():
            load_second(1)

        return 0

    lax.fori_loop(0, 2, forward_layer, 0)
    gather.drain()

    def backward_layer(turn, _):
        layer = 1 - turn
        again = turn > 0
        second, dense, attention = (Tensor(turn, which) for which in range(3))
        _, dense_before, attention_before = (Tensor(turn - 1, which) for which in range(3))
        body.enter(layer, 1)

        @pl.when(again)
        def _():
            reduce.prepare(second, dense_before)

        body.second_half(second, False)

        @pl.when(again)
        def _():
            reduce.third(dense_before)
            loaded_second(0)

        body.down(layer)

        @pl.when(turn == 0)
        def _():
            load_second(0)

        @pl.when(again)
        def _():
            reduce.merge(attention_before)

        body.second_half(second, True)
        reduce.first(second)

        @pl.when(again)
        def _():
            reduce.second(attention_before)
            reduce.prepare(dense, attention_before)

        body.first_half(dense, False)

        @pl.when(again)
        def _():
            reduce.close(dense_before)

        body.leave(layer, 1)
        reduce.merge(second)
        body.first_half(dense, True)
        reduce.first(dense)
        body.enter(layer, 0)
        body.back_out(layer)

        @pl.when(again)
        def _():
            reduce.third(attention_before)

        body.pairs(layer, 0)
        reduce.second(second)
        reduce.merge(dense)
        body.pairs(layer, 1)

        @pl.when(again)
        def _():
            reduce.close(attention_before)

        reduce.prepare(attention, second)
        body.first_half(attention, False)
        reduce.third(second)
        body.fold_bias(layer)
        body.leave(layer, 0)
        reduce.second(dense)
        body.first_half(attention, True)
        reduce.first(attention)
        reduce.close(second)
        return 0

    lax.fori_loop(0, 2, backward_layer, 0)
    dense, attention = Tensor(1, 1), Tensor(1, 2)
    grad = g[...].astype(F32)
    tokens_grad[0] = (grad * (1.0 - here)).astype(BF16)[:SEQ]
    small[20:21, :] = jnp.sum(grad * here, axis=0, keepdims=True)
    small[21:24, :] = jnp.zeros((3, D), F32)
    sums.start(small)
    reduce.third(dense)
    sums.step(0)
    reduce.merge(attention)
    sums.step(1)
    reduce.close(dense)
    reduce.second(attention)
    sums.step(2)
    reduce.third(attention)
    sums.step(3)
    reduce.close(attention)
    sums.close(totals)
    Share(place, first_out, w.at[3], share_sems).run(first_grad, share_out_sems)
    reduce.finish()


def layers(tokens, masked, cotangent, live, mask_token, norm_gain, norm_shift, layer_scale, w_own, w2, tables):
    vm = pl.BlockSpec(memory_space=pltpu.VMEM)
    hbm = pl.BlockSpec(memory_space=pl.ANY)
    sm = pl.BlockSpec(memory_space=pltpu.SMEM)
    V, DMA, REGULAR = pltpu.VMEM, pltpu.SemaphoreType.DMA, pltpu.SemaphoreType.REGULAR
    return pl.pallas_call(
        layers_kernel,
        out_shape=(
            jax.ShapeDtypeStruct((1, SEQ, D), BF16),
            jax.ShapeDtypeStruct((1, SEQ, D), BF16),
            jax.ShapeDtypeStruct((4, 4, 48, FF), BF16),
            jax.ShapeDtypeStruct((2, 24, D), F32),
            jax.ShapeDtypeStruct((48, D), F32),
        ),
        in_specs=[vm, vm, vm, sm, vm, vm, vm, vm, hbm, hbm, vm],
        out_specs=(vm, vm, hbm, vm, vm),
        scratch_shapes=[
            V((4, 4, 4, 48, FF), BF16), V((FF, D), BF16), V((4, ROWS, D), BF16), V((2, KEYS, 2304), BF16),
            V((2, HEADS, 16 * GRID, KEYS), BF16), V((2, ROWS, D), BF16), V((2, ROWS, FF), BF16), V((2, ROWS, FF), BF16),
            V((4, ROWS, D), BF16), V((2, ROWS, D), BF16), V((2, HEADS, ROWS, KEYS), BF16), V((2 * HEADS, 896), F32), V((384, KEYS), BF16),
            V((16 * GRID, ROWS), BF16),
            V((3, ROWS, 128), F32), V((ROWS, FF), BF16), V((ROWS, D), BF16), V((ROWS, D), BF16),
            V((8, D), F32), V((4, 8, D), F32), V((48, D), F32),
            V((2,) + HALF, BF16), V((2,) + HALF, BF16), V((2, 3, 6, 2, 4, 16, 384), BF16),
            V((2, 3, 4, 4, 16, 384), BF16), V((2, 3, 3, 4, 16, 384), BF16),
            V((2, 3, 4, 16, 384), BF16), V((6, 3, 3, 16, 384), BF16),
            V((2, 2, 24, 384), F32), V((2, 24, 384), F32), V((24, D), F32), V((14, 24, D), F32),
            V((4, 1, 1, 3, 16, 384), BF16),
            DMA((2, 8)), DMA((8,)), DMA((2, GATHER_MESSAGES)), DMA((2, 6, 43)), DMA((2, 11)), DMA((2, 75)), DMA((48,)), REGULAR, REGULAR((3, 2)),
        ],
        compiler_params=pltpu.CompilerParams(
            collective_id=1, has_side_effects=True, vmem_limit_bytes=64 * 2**20
        ),
    )(tokens, masked, cotangent, live, mask_token, norm_gain, norm_shift, layer_scale, w_own, w2, tables)


class Share(Spread):
    def __init__(self, place, blocks, full, sems):
        super().__init__(place, sems)
        self.blocks, self.full = blocks, full

    def regions(self, c, x, y, z):
        def columns(third):
            return pl.ds(pl.multiple_of((c * 4 + third[0]) * 384, 128), third[1] * 384)

        for route, (a1, a2, a3) in enumerate(((x, y, z), (y, z, x), (z, x, y))):
            yield route, self.full.at[
                pl.ds(*a1), pl.ds(*a2), slice(16 * route, 16 * route + 16), columns(a3)
            ]

    def pass_on(self, base, regions, device):
        for route, region in regions:
            self.send(base + route, region, region, device)

    def await_all(self, base, regions):
        for route, region in regions:
            self.wait(base + route, region)

    def keep(self, out, c, x, y, z):
        for (route, region), (_, target) in zip(self.regions(c, x, y, z), Share(self.place, None, out, None).regions(c, x, y, z)):
            copy = pltpu.make_async_copy(region, target, self.out_sems.at[len(self.kept)])
            copy.start()
            self.kept.append(copy)

    def run(self, out, out_sems):
        place = self.place
        at = place.at
        self.out_sems, self.kept = out_sems, []
        c, x, y, z = at["c"], (at["x"], 1), (at["y"], 1), (at["z"], 1)
        other = 1 - c
        every = (0, 4)
        halves = ((0, 2), (2, 2))

        def near(axis, step):
            return (place.index(axis, step), 1)

        for route, region in self.regions(c, x, y, z):
            for step in (1, 2, 3):
                source = self.blocks.at[place.index("y", step), :, :, route]
                self.send(3 * (step - 1) + route, source, region, place.go("y", step))
            region[...] = self.blocks[at["y"], :, :, route]
        for step in (1, 2, 3):
            self.await_all(3 * (step - 1), self.regions(c, x, near("y", 4 - step), z))
        for step in (1, 3, 2):
            self.pass_on(9 + 3 * (step - 1), self.regions(c, x, halves[0], z), place.go("x", step))
            self.pass_on(18 + 3 * (step - 1), self.regions(c, x, halves[1], z), place.go("z", step))
        for step in (1, 3, 2):
            self.await_all(9 + 3 * (step - 1), self.regions(c, near("x", 4 - step), halves[0], z))
            self.await_all(18 + 3 * (step - 1), self.regions(c, x, halves[1], near("z", 4 - step)))
        for step in (1, 3):
            self.pass_on(27 + 3 * (step - 1), self.regions(c, every, halves[0], z), place.go("z", step))
            self.pass_on(36 + 3 * (step - 1), self.regions(c, x, halves[1], every), place.go("x", step))
        self.pass_on(45, self.regions(c, every, halves[0], z), place.go("c", 1))
        self.pass_on(48, self.regions(c, x, halves[1], every), place.go("c", 1))
        self.keep(out, c, every, halves[0], z)
        self.keep(out, c, x, halves[1], every)
        for step, part, base in ((1, (0, 1), 30), (3, (1, 1), 69)):
            self.await_all(27 + 3 * (step - 1), self.regions(c, every, halves[0], near("z", 4 - step)))
            self.pass_on(base, self.regions(c, every, part, near("z", 4 - step)), place.go("z", step))
            part = (part[0] + 2, 1)
            self.await_all(36 + 3 * (step - 1), self.regions(c, near("x", 4 - step), halves[1], every))
            self.pass_on(base + (9 if base == 30 else 3), self.regions(c, near("x", 4 - step), part, every), place.go("x", step))
        for step in (1, 3):
            self.pass_on(51 + 3 * (step - 1), self.regions(c, every, halves[0], near("z", 4 - step)), place.go("c", 1))
            self.pass_on(60 + 3 * (step - 1), self.regions(c, near("x", 4 - step), halves[1], every), place.go("c", 1))
            self.keep(out, c, every, halves[0], near("z", 4 - step))
            self.keep(out, c, near("x", 4 - step), halves[1], every)
        self.await_all(45, self.regions(other, every, halves[0], z))
        self.keep(out, other, every, halves[0], z)
        self.await_all(48, self.regions(other, x, halves[1], every))
        self.keep(out, other, x, halves[1], every)
        for step in (1, 3):
            self.await_all(51 + 3 * (step - 1), self.regions(other, every, halves[0], near("z", 4 - step)))
            self.keep(out, other, every, halves[0], near("z", 4 - step))
            self.await_all(60 + 3 * (step - 1), self.regions(other, near("x", 4 - step), halves[1], every))
            self.keep(out, other, near("x", 4 - step), halves[1], every)
        for part, base in ((0, 30), (1, 69)):
            self.await_all(base, self.regions(c, every, (part, 1), near("z", 2)))
            self.await_all(base + (9 if base == 30 else 3), self.regions(c, near("x", 2), (part + 2, 1), every))
        self.pass_on(54, self.regions(c, every, halves[0], near("z", 2)), place.go("c", 1))
        self.pass_on(63, self.regions(c, near("x", 2), halves[1], every), place.go("c", 1))
        self.keep(out, c, every, halves[0], near("z", 2))
        self.keep(out, c, near("x", 2), halves[1], every)
        self.await_all(54, self.regions(other, every, halves[0], near("z", 2)))
        self.keep(out, other, every, halves[0], near("z", 2))
        self.await_all(63, self.regions(other, near("x", 2), halves[1], every))
        self.keep(out, other, near("x", 2), halves[1], every)
        for copy in self.kept:
            copy.wait()
        self.drain()


def finish_kernel(
    first, block_in, tokens_in, second_in, totals, live,
    block_out, tokens_grad, first_grad, second_grad, gain_grad, shift_grad, scale_grad, table_grad, mask_grad, rms_out,
    narrow, wide, load_sems, store_sems,
):
    loads, stores = [], []
    for block in range(16):
        a1, a2 = block // 4, block % 4
        rows = pl.ds(block * 48, 48)
        loads.append(pltpu.make_async_copy(first.at[a1, a2], narrow.at[a1, a2], load_sems.at[block]))
        stores.append(pltpu.make_async_copy(wide.at[rows], first_grad.at[0, rows], store_sems.at[block]))
    for load in loads:
        load.start()
    for block in range(16):
        loads[block].wait()
        wide[block * 48 : block * 48 + 48, :] = narrow[block // 4, block % 4].astype(F32)
        stores[block].start()
    block_out[...] = block_in[...]
    tokens_grad[...] = tokens_in[...]
    second_grad[...] = second_in[...]
    own = 8 + 3 * lax.axis_index("section")
    scale_grad[...] = totals[pl.ds(own, 1), :]
    gain_grad[...] = totals[pl.ds(own + 1, 1), :]
    shift_grad[...] = totals[pl.ds(own + 2, 1), :]
    mask_grad[...] = totals[20, :]
    count = lax.fori_loop(0, live.shape[0], lambda i, total: total + live[i], 0)
    tokens = count.astype(F32) * (SEQ * D)
    rms = jnp.sqrt(jnp.sum(totals[0:8, :], axis=1, keepdims=True) / tokens)
    rms_out[...] = jnp.concatenate(
        [jnp.concatenate([rms[2 * s + k : 2 * s + k + 1] for s in range(4)], axis=1) for k in range(2)], axis=0
    )
    for layer in range(2):
        table_grad[:, layer, :] = totals[24 + layer * HEADS : 24 + (layer + 1) * HEADS, : table_grad.shape[2]]
    for store in stores:
        store.wait()


def finish_all(first, block_out, tokens_grad, second, totals, live, entries):
    vm = pl.BlockSpec(memory_space=pltpu.VMEM)
    hbm = pl.BlockSpec(memory_space=pl.ANY)
    image, pair, vector = (1, SEQ, D), (2, 24, D), (1, D)
    return pl.pallas_call(
        finish_kernel,
        out_shape=(
            jax.ShapeDtypeStruct(image, BF16), jax.ShapeDtypeStruct(image, BF16), jax.ShapeDtypeStruct((1, D, FF), F32),
            jax.ShapeDtypeStruct(pair, F32), jax.ShapeDtypeStruct(vector, F32), jax.ShapeDtypeStruct(vector, F32),
            jax.ShapeDtypeStruct(vector, F32), jax.ShapeDtypeStruct((HEADS, 2, entries), F32),
            jax.ShapeDtypeStruct((D,), F32), jax.ShapeDtypeStruct((2, 4), F32),
        ),
        in_specs=[hbm, vm, vm, vm, vm, pl.BlockSpec(memory_space=pltpu.SMEM)],
        out_specs=(vm, vm, hbm) + (vm,) * 7,
        scratch_shapes=[
            pltpu.VMEM((4, 4, 48, FF), BF16), pltpu.VMEM((D, FF), F32),
            pltpu.SemaphoreType.DMA((16,)), pltpu.SemaphoreType.DMA((16,)),
        ],
        compiler_params=pltpu.CompilerParams(vmem_limit_bytes=62 * 2**20),
    )(first, block_out, tokens_grad, second, totals, live)


def on_device(
    tokens, masked, live_images, mask_token, norm_gain, norm_shift, w_first, w_second, layer_scale, rel_table, cotangent
):
    block_out, tokens_grad, first, second, totals = layers(
        tokens, masked, cotangent, live_images, mask_token, norm_gain, norm_shift, layer_scale, w_first, w_second,
        jnp.transpose(rel_table, (2, 0, 1)),
    )
    *outs, table_grad, mask_grad, rms = finish_all(
        first, block_out, tokens_grad, second, totals, live_images, rel_table.shape[1]
    )
    return (*outs, jnp.transpose(table_grad, (1, 2, 0)), mask_grad, rms.T)


def solution(mesh):
    both = P(("dp", "section"), None, None)
    part = P("section", None)
    return jax.shard_map(
        on_device,
        mesh=mesh,
        in_specs=(both, P(("dp", "section"), None), P(), P(), part, part, P("section", None, None), P(), part, P(), both),
        out_specs=(
            both, both, P("section", None, None), P(None, ("dp", "section"), None), part, part, part, P(), P(), P(),
        ),
        check_vma=False,
    )
```

profile of v0, /device:TPU:1, one launch (start us, length us, event | category | flops | bytes accessed | tf_op | source)
XLA Modules:
  0.0 196.1 jit_solution(1462107221793602523)
XLA Ops:
  0.6 188.4 %shard_map.186 = (bf16[1,197,768]{2,1,0:T(8,128)(2,1)}, bf16[1,197,768]{2,1,0:T(8,128)(2,1)}, bf16[4,4,48,3072]{3,2,1,0:T(8,128)(2,1)}, f32[2,24,768]{2,1,0:T(8,128)}, f32[48,768]{1,0:T(8,128)}) custom-call(bf16[1,197,768]{2,1,0:T(8,128)(2,1)} %tokens.1, s32[1,197]{1,0:T(1,128)} %masked.1, bf16[1,197,768]{2,1,0:T(8,128)(2,1)} %cotangent.1, s32[32]{0:T(128)} %live.3, ...), custom_call_target="tpu_custom_call" | custom-call | tf_op jit(solution)/shard_map/pallas_call | solution.py:986
  189.0 6.9 %shard_map.187 = (bf16[1,197,768]{2,1,0:T(8,128)(2,1)}, bf16[1,197,768]{2,1,0:T(8,128)(2,1)}, f32[1,768,3072]{2,1,0:T(8,128)}, f32[2,24,768]{2,1,0:T(8,128)}, f3...) custom-call(bf16[4,4,48,3072]{3,2,1,0:T(8,128)(2,1)} %get-tuple-elem, ...), custom_call_target="tpu_custom_call" | custom-call | tf_op jit(solution)/shard_map/pallas_call | solution.py:1154
where the time goes:
time: 196 us
  Pallas kernels  195 us (99%)
    pallas_call x1, Pallas kernels, layers(): pl.pallas_call(layers_kernel, out_shape=(jax.ShapeDtypeStruct((1, SEQ, D)...  188 us
    pallas_call x1, Pallas kernels, finish_all(): pl.pallas_call(finish_kernel, out_shape=(jax.ShapeDtypeStruct(image, BF16...  6.95 us

commit v1 on v0

--- a/solution.py
+++ b/solution.py
@@ -589,33 +589,31 @@
         for copy in self.now:
             copy.wait_recv()
         if number == 0:
-            self.part[...] = self.small[self.half(me), :] + self.bufs[12]
+            self.part[0] = self.small[self.half(me), :] + self.bufs[12]
         else:
             axis = AXES[number - 1]
-            self.bufs[4 * number - 4 + place.at[axis]] = self.part[...]
-            self.part[...] = (
+            self.bufs[4 * number - 4 + place.at[axis]] = self.part[number - 1]
+            self.part[number] = (
                 (self.bufs[4 * number - 4] + self.bufs[4 * number - 3])
                 + (self.bufs[4 * number - 2] + self.bufs[4 * number - 1])
             )
         if number < 3:
             axis = AXES[number]
             self.now = [
-                self.send(self.part, self.bufs.at[4 * number + place.at[axis]], 1 + 3 * number + step - 1, place.go(axis, step))
+                self.send(self.part.at[number], self.bufs.at[4 * number + place.at[axis]], 1 + 3 * number + step - 1, place.go(axis, step))
                 for step in (1, 2, 3)
             ]
-            for copy in self.now:
-                copy.wait_send()
         else:
-            self.now = [self.send(self.part, self.bufs.at[13], 10, place.go("c", 1))]
+            self.now = [self.send(self.part.at[3], self.bufs.at[13], 10, place.go("c", 1))]
 
     def close(self, out):
         me = self.place.at["c"]
         for copy in self.now:
             copy.wait_recv()
-        out[self.half(me), :] = self.part[...]
+        out[self.half(me), :] = self.part[3]
         out[self.half(1 - me), :] = self.bufs[13]
-        self.copies[0].wait_send()
-        self.copies[-1].wait_send()
+        for copy in self.copies:
+            copy.wait_send()
 
 
 class Spread:
@@ -690,9 +688,7 @@
                 (rest if block else mine).append(copy)
         for copy in mine + rest:
             copy.start()
-        for copy in mine:
-            copy.wait()
-        return rest
+        return mine, rest
 
     def own(self, up, down):
         copies = []
@@ -766,17 +762,25 @@
     block_out, tokens_grad, first_grad, second_out, totals,
     w, w2, h, qkv, probs, o, a, slope, p, n, bias, table, select_f, by_x, fold_sums, du, dp, g, vec, vecs, small,
     stage, pair, far, line, line_in, spot, spot_in, rows, rows_in, part, bufs, first_out,
-    load_sems, w2_sems, gather_sems, sems, small_sems, share_sems, share_out_sems, pair_credit, far_credit,
+    tokens_in, cotangent_in, load_sems, w2_sems, image_sems, gather_sems, sems, small_sems, share_sems, share_out_sems, pair_credit, far_credit,
 ):
     place = Place()
     vec[0:1] = norm_gain[...]
     vec[1:2] = norm_shift[...]
     vec[2:3] = layer_scale[...]
     vec[3:8] = jnp.zeros((5, D), F32)
-    meet(place)
     y = place.at["y"]
     gather = Gather(place, w, gather_sems)
-    own_rest = gather.load(w_own.at[0], load_sems)
+    own_first, own_rest = gather.load(w_own.at[0], load_sems)
+    images = [
+        pltpu.make_async_copy(source, target, image_sems.at[i])
+        for i, (source, target) in enumerate(((tokens, tokens_in), (cotangent, cotangent_in)))
+    ]
+    for copy in images:
+        copy.start()
+    meet(place)
+    for copy in own_first:
+        copy.wait()
     for copy in gather.own("x", "z"):
         copy.start()
     own_later = gather.own("z", "x")
@@ -812,7 +816,7 @@
     valid = jnp.where(y < live[lax.axis_index("dp")], 1.0, 0.0)
     body = Body(
         valid=valid, core=place.at["c"], vecs=vecs, table=table,
-        select_forward=select_f, by_x=by_x, block_out=block_out, small=small,
+        select_forward=select_f, by_x=by_x, block_out=tokens_in, small=small,
         w=w, w2=w2, h=h, qkv=qkv, probs=probs, o=o, a=a, slope=slope, p=p, n=n, bias=bias,
         sums=fold_sums, du=du, dp=dp, g=g, stage=stage, pair=pair,
     )
@@ -837,10 +841,12 @@
     flags = jnp.concatenate([masked[...].astype(F32), jnp.zeros((1, KEYS - SEQ), F32)], axis=1)
     here = jnp.sum(jnp.where(diagonal, flags, 0.0), axis=1, keepdims=True)
     h[0, 192:] = jnp.zeros((16, D), BF16)
-    start = tokens[0].astype(F32)
+    for copy in images:
+        copy.wait()
+    start = tokens_in[0].astype(F32)
     h[0, :SEQ] = (start + here[:SEQ] * (mask_token[...].astype(F32).reshape(1, D) - start)).astype(BF16)
     g[192:] = jnp.zeros((16, D), BF16)
-    g[:SEQ] = (cotangent[0].astype(F32) * valid).astype(BF16)
+    g[:SEQ] = (cotangent_in[0].astype(F32) * valid).astype(BF16)
     body.make_selectors()
     body.read_tables(tables)
     body.expand_bias(0, 0, 6)
@@ -881,6 +887,8 @@
         return 0
 
     lax.fori_loop(0, 2, forward_layer, 0)
+    block_copy = pltpu.make_async_copy(tokens_in, block_out, image_sems.at[0])
+    block_copy.start()
     gather.drain()
 
     def backward_layer(turn, _):
@@ -938,8 +946,8 @@
 
         body.pairs(layer, 0)
         reduce.second(second)
+        body.pairs(layer, 1)
         reduce.merge(dense)
-        body.pairs(layer, 1)
 
         @pl.when(again)
         def _():
@@ -947,8 +955,8 @@
 
         reduce.prepare(attention, second)
         body.first_half(attention, False)
+        body.fold_bias(layer)
         reduce.third(second)
-        body.fold_bias(layer)
         body.leave(layer, 0)
         reduce.second(dense)
         body.first_half(attention, True)
@@ -959,23 +967,25 @@
     lax.fori_loop(0, 2, backward_layer, 0)
     dense, attention = Tensor(1, 1), Tensor(1, 2)
     grad = g[...].astype(F32)
-    tokens_grad[0] = (grad * (1.0 - here)).astype(BF16)[:SEQ]
+    cotangent_in[0] = (grad * (1.0 - here)).astype(BF16)[:SEQ]
+    tokens_copy = pltpu.make_async_copy(cotangent_in, tokens_grad, image_sems.at[1])
+    tokens_copy.start()
     small[20:21, :] = jnp.sum(grad * here, axis=0, keepdims=True)
     small[21:24, :] = jnp.zeros((3, D), F32)
     sums.start(small)
     reduce.third(dense)
-    sums.step(0)
     reduce.merge(attention)
-    sums.step(1)
     reduce.close(dense)
     reduce.second(attention)
-    sums.step(2)
+    sums.step(0)
     reduce.third(attention)
-    sums.step(3)
+    sums.step(1)
     reduce.close(attention)
-    sums.close(totals)
-    Share(place, first_out, w.at[3], share_sems).run(first_grad, share_out_sems)
+    beside = [lambda: sums.step(2), lambda: sums.step(3), lambda: sums.close(totals)]
+    Share(place, first_out, w.at[3], share_sems).run(first_grad, share_out_sems, beside)
     reduce.finish()
+    block_copy.wait()
+    tokens_copy.wait()
 
 
 def layers(tokens, masked, cotangent, live, mask_token, norm_gain, norm_shift, layer_scale, w_own, w2, tables):
@@ -992,8 +1002,8 @@
             jax.ShapeDtypeStruct((2, 24, D), F32),
             jax.ShapeDtypeStruct((48, D), F32),
         ),
-        in_specs=[vm, vm, vm, sm, vm, vm, vm, vm, hbm, hbm, vm],
-        out_specs=(vm, vm, hbm, vm, vm),
+        in_specs=[hbm, vm, hbm, sm, vm, vm, vm, vm, hbm, hbm, vm],
+        out_specs=(hbm, hbm, hbm, vm, vm),
         scratch_shapes=[
             V((4, 4, 4, 48, FF), BF16), V((FF, D), BF16), V((4, ROWS, D), BF16), V((2, KEYS, 2304), BF16),
             V((2, HEADS, 16 * GRID, KEYS), BF16), V((2, ROWS, D), BF16), V((2, ROWS, FF), BF16), V((2, ROWS, FF), BF16),
@@ -1004,9 +1014,9 @@
             V((2,) + HALF, BF16), V((2,) + HALF, BF16), V((2, 3, 6, 2, 4, 16, 384), BF16),
             V((2, 3, 4, 4, 16, 384), BF16), V((2, 3, 3, 4, 16, 384), BF16),
             V((2, 3, 4, 16, 384), BF16), V((6, 3, 3, 16, 384), BF16),
-            V((2, 2, 24, 384), F32), V((2, 24, 384), F32), V((24, D), F32), V((14, 24, D), F32),
-            V((4, 1, 1, 3, 16, 384), BF16),
-            DMA((2, 8)), DMA((8,)), DMA((2, GATHER_MESSAGES)), DMA((2, 6, 43)), DMA((2, 11)), DMA((2, 75)), DMA((48,)), REGULAR, REGULAR((3, 2)),
+            V((2, 2, 24, 384), F32), V((2, 24, 384), F32), V((4, 24, D), F32), V((14, 24, D), F32),
+            V((4, 1, 1, 3, 16, 384), BF16), V((1, SEQ, D), BF16), V((1, SEQ, D), BF16),
+            DMA((2, 8)), DMA((8,)), DMA((2,)), DMA((2, GATHER_MESSAGES)), DMA((2, 6, 43)), DMA((2, 11)), DMA((2, 75)), DMA((48,)), REGULAR, REGULAR((3, 2)),
         ],
         compiler_params=pltpu.CompilerParams(
             collective_id=1, has_side_effects=True, vmem_limit_bytes=64 * 2**20
@@ -1042,7 +1052,7 @@
             copy.start()
             self.kept.append(copy)
 
-    def run(self, out, out_sems):
+    def run(self, out, out_sems, beside):
         place = self.place
         at = place.at
         self.out_sems, self.kept = out_sems, []
@@ -1059,11 +1069,13 @@
                 source = self.blocks.at[place.index("y", step), :, :, route]
                 self.send(3 * (step - 1) + route, source, region, place.go("y", step))
             region[...] = self.blocks[at["y"], :, :, route]
+        beside[0]()
         for step in (1, 2, 3):
             self.await_all(3 * (step - 1), self.regions(c, x, near("y", 4 - step), z))
         for step in (1, 3, 2):
             self.pass_on(9 + 3 * (step - 1), self.regions(c, x, halves[0], z), place.go("x", step))
             self.pass_on(18 + 3 * (step - 1), self.regions(c, x, halves[1], z), place.go("z", step))
+        beside[1]()
         for step in (1, 3, 2):
             self.await_all(9 + 3 * (step - 1), self.regions(c, near("x", 4 - step), halves[0], z))
             self.await_all(18 + 3 * (step - 1), self.regions(c, x, halves[1], near("z", 4 - step)))
@@ -1074,6 +1086,7 @@
         self.pass_on(48, self.regions(c, x, halves[1], every), place.go("c", 1))
         self.keep(out, c, every, halves[0], z)
         self.keep(out, c, x, halves[1], every)
+        beside[2]()
         for step, part, base in ((1, (0, 1), 30), (3, (1, 1), 69)):
             self.await_all(27 + 3 * (step - 1), self.regions(c, every, halves[0], near("z", 4 - step)))
             self.pass_on(base, self.regions(c, every, part, near("z", 4 - step)), place.go("z", step))
@@ -1113,9 +1126,15 @@
 def finish_kernel(
     first, block_in, tokens_in, second_in, totals, live,
     block_out, tokens_grad, first_grad, second_grad, gain_grad, shift_grad, scale_grad, table_grad, mask_grad, rms_out,
-    narrow, wide, load_sems, store_sems,
+    narrow, wide, images, load_sems, store_sems, image_sems,
 ):
     loads, stores = [], []
+    through = []
+    for i, (source, target) in enumerate(((block_in, block_out), (tokens_in, tokens_grad))):
+        through.append((
+            pltpu.make_async_copy(source, images.at[i], image_sems.at[i]),
+            pltpu.make_async_copy(images.at[i], target, image_sems.at[2 + i]),
+        ))
     for block in range(16):
         a1, a2 = block // 4, block % 4
         rows = pl.ds(block * 48, 48)
@@ -1123,12 +1142,15 @@
         stores.append(pltpu.make_async_copy(wide.at[rows], first_grad.at[0, rows], store_sems.at[block]))
     for load in loads:
         load.start()
+    for load, _ in through:
+        load.start()
     for block in range(16):
         loads[block].wait()
         wide[block * 48 : block * 48 + 48, :] = narrow[block // 4, block % 4].astype(F32)
         stores[block].start()
-    block_out[...] = block_in[...]
-    tokens_grad[...] = tokens_in[...]
+    for load, store in through:
+        load.wait()
+        store.start()
     second_grad[...] = second_in[...]
     own = 8 + 3 * lax.axis_index("section")
     scale_grad[...] = totals[pl.ds(own, 1), :]
@@ -1145,6 +1167,8 @@
         table_grad[:, layer, :] = totals[24 + layer * HEADS : 24 + (layer + 1) * HEADS, : table_grad.shape[2]]
     for store in stores:
         store.wait()
+    for _, store in through:
+        store.wait()
 
 
 def finish_all(first, block_out, tokens_grad, second, totals, live, entries):
@@ -1159,11 +1183,11 @@
             jax.ShapeDtypeStruct(vector, F32), jax.ShapeDtypeStruct((HEADS, 2, entries), F32),
             jax.ShapeDtypeStruct((D,), F32), jax.ShapeDtypeStruct((2, 4), F32),
         ),
-        in_specs=[hbm, vm, vm, vm, vm, pl.BlockSpec(memory_space=pltpu.SMEM)],
-        out_specs=(vm, vm, hbm) + (vm,) * 7,
+        in_specs=[hbm, hbm, hbm, vm, vm, pl.BlockSpec(memory_space=pltpu.SMEM)],
+        out_specs=(hbm, hbm, hbm) + (vm,) * 7,
         scratch_shapes=[
-            pltpu.VMEM((4, 4, 48, FF), BF16), pltpu.VMEM((D, FF), F32),
-            pltpu.SemaphoreType.DMA((16,)), pltpu.SemaphoreType.DMA((16,)),
+            pltpu.VMEM((4, 4, 48, FF), BF16), pltpu.VMEM((D, FF), F32), pltpu.VMEM((2, 1, SEQ, D), BF16),
+            pltpu.SemaphoreType.DMA((16,)), pltpu.SemaphoreType.DMA((16,)), pltpu.SemaphoreType.DMA((4,)),
         ],
         compiler_params=pltpu.CompilerParams(vmem_limit_bytes=62 * 2**20),
     )(first, block_out, tokens_grad, second, totals, live)

time: 196 us -> 190 us (0.969)
  Pallas kernels: 195 us -> 189 us
    pallas_call x1, Pallas kernels: 188 us -> 182 us  [layers(): pl.pallas_call(layers_kernel, out_shape=(jax.ShapeDtypeStruct((1, SEQ, D)...]
where the time goes in v1:
time: 190 us
  Pallas kernels  189 us (99%)
    pallas_call x1, Pallas kernels, layers(): pl.pallas_call(layers_kernel, out_shape=(jax.ShapeDtypeStruct((1, SEQ, D)...  182 us
    pallas_call x1, Pallas kernels, finish_all(): pl.pallas_call(finish_kernel, out_shape=(jax.ShapeDtypeStruct(image, BF16...  6.9 us

profile of v1, /device:TPU:1, one launch (start us, length us, event | category | flops | bytes accessed | tf_op | source)
XLA Modules:
  0.0 190.1 jit_solution(18441323738203118793)
XLA Ops:
  0.6 182.4 %shard_map.186 = (bf16[1,197,768]{2,1,0:T(8,128)(2,1)}, bf16[1,197,768]{2,1,0:T(8,128)(2,1)}, bf16[4,4,48,3072]{3,2,1,0:T(8,128)(2,1)}, f32[2,24,768]{2,1,0:T(8,128)}, f32[48,768]{1,0:T(8,128)}) custom-call(bf16[1,197,768]{2,1,0:T(8,128)(2,1)} %tokens.1, s32[1,197]{1,0:T(1,128)} %masked.1, bf16[1,197,768]{2,1,0:T(8,128)(2,1)} %cotangent.1, s32[32]{0:T(128)} %live.3, ...), custom_call_target="tpu_custom_call" | custom-call | tf_op jit(solution)/shard_map/pallas_call | solution.py:996
  183.1 6.9 %shard_map.187 = (bf16[1,197,768]{2,1,0:T(8,128)(2,1)}, bf16[1,197,768]{2,1,0:T(8,128)(2,1)}, f32[1,768,3072]{2,1,0:T(8,128)}, f32[2,24,768]{2,1,0:T(8,128)}, f3...) custom-call(bf16[4,4,48,3072]{3,2,1,0:T(8,128)(2,1)} %get-tuple-elem, ...), custom_call_target="tpu_custom_call" | custom-call | tf_op jit(solution)/shard_map/pallas_call | solution.py:1178

commit v2 on v1

--- a/solution.py
+++ b/solution.py
@@ -136,14 +136,7 @@
         self.p[s] = projected.astype(BF16)
         self.note(2 * s, jnp.sum(branch * branch * real, axis=0, keepdims=True))
         self.note(2 * s + 1, jnp.sum(result * result * real, axis=0, keepdims=True))
-
-        @pl.when(s < 3)
-        def _():
-            self.h[s + 1] = result.astype(BF16)
-
-        @pl.when(s == 3)
-        def _():
-            self.block_out[0] = (result[:SEQ] * self.valid).astype(BF16)
+        self.h[s + 1] = result.astype(BF16)
 
     def attend_forward(self, layer):
         s = 2 * layer
@@ -171,7 +164,7 @@
                 probs = (exps * (1.0 / total)).astype(BF16)
                 self.probs[layer, 2 * j + parity, :ROWS] = probs
                 mixed = mixed + mm(probs, keep_half(v, parity))
-            self.o[layer, :, lanes(j * 128, 128)] = mixed.astype(BF16)
+            self.n[1 + layer, :, lanes(j * 128, 128)] = mixed.astype(BF16)
 
         def pairs(i, _):
             for j in range(3):
@@ -179,7 +172,7 @@
             return 0
 
         lax.fori_loop(0, 2, pairs, 0)
-        self.finish(s, self.o.at[layer], self.w[s, :, :, :, 2304:].reshape(D, D))
+        self.finish(s, self.n.at[1 + layer], self.w[s, :, :, :, 2304:].reshape(D, D))
 
     def dense_forward(self, layer):
         s = 2 * layer + 1
@@ -194,18 +187,30 @@
             return 0
 
         lax.fori_loop(0, 3, up, 0)
-        self.finish(s, self.a.at[layer], self.w2[...])
+
+    def last_finish(self):
+        real = (lax.broadcasted_iota(jnp.int32, (ROWS, 1), 0) < SEQ).astype(F32) * self.valid
+
+        def block(j, _):
+            columns = lanes(j * 384, 384)
+            projected = mm(self.a[1], self.w2[:, columns])
+            branch = self.vecs[3, 2:3, columns] * projected
+            result = self.h[3, :, columns].astype(F32) + branch
+            self.p[3, :, columns] = projected.astype(BF16)
+            self.small[6:7, columns] = jnp.sum(branch * branch * real, axis=0, keepdims=True)
+            self.small[7:8, columns] = jnp.sum(result * result * real, axis=0, keepdims=True)
+            self.block_out[0, :, columns] = (result[:SEQ] * self.valid).astype(BF16)
+            return 0
+
+        lax.fori_loop(0, 2, block, 0)
 
     def enter(self, layer, dense):
         s = 2 * layer + dense
         g = self.g[...].astype(F32)
-        row = 8 + 3 * s
-        self.note(row, jnp.sum(g * self.p[s].astype(F32), axis=0, keepdims=True))
         dp = (g * self.vecs[s, 2:3, :]).astype(BF16)
         self.dp[...] = dp
         self.normed(s)
         if not dense:
-            self.n[1] = self.o[layer]
             self.du[:, 2304:] = dp
 
     def leave(self, layer, dense):
@@ -214,12 +219,14 @@
         dn = mm_nt(self.du[:, :width], self.w[s, :, :, :, :width].reshape(D, width))
         scaled, inv_std = centre(self.h[s].astype(F32))
         row = 8 + 3 * s
+        g = self.g[...].astype(F32)
+        self.note(row, jnp.sum(g * self.p[s].astype(F32), axis=0, keepdims=True))
         self.note(row + 1, jnp.sum(dn * scaled, axis=0, keepdims=True))
         self.note(row + 2, jnp.sum(dn, axis=0, keepdims=True))
         e = dn * self.vecs[s, 0:1, :]
         mean_e = jnp.mean(e, axis=-1, keepdims=True)
         mean_ex = jnp.mean(e * scaled, axis=-1, keepdims=True)
-        g = self.g[...].astype(F32) + inv_std * (e - mean_e - scaled * mean_ex)
+        g = g + inv_std * (e - mean_e - scaled * mean_ex)
         self.g[...] = g.astype(BF16)
 
     def put(self, t, mine, route, a1, a2, a3, piece):
@@ -236,7 +243,7 @@
             if mine:
                 self.reduce.swapped(t, i)
             j = half * 2 + i
-            left = jnp.where(j == 3, 1, 0) if t.which == 2 else 0
+            left = jnp.where(j == 3, 1 + t.layer, 0) if t.which == 2 else 0
             grad = mm_tn(self.n[left], self.du[:, lanes(j * 768, 768)])
             for side in range(2):
                 for rb in range(16):
@@ -432,7 +439,7 @@
     def spot_copy(self, t, r, step):
         axis = ROUTES[r][2]
         source = self.spot.at[t.slot, r, self.place.index(axis, step)]
-        return self.link(t, 32 + 3 * r + step, source, self.spot_in.at[t.number, r, step - 1], self.place.go(axis, step))
+        return self.link(t, 32 + 3 * r + step, source, self.spot_in.at[t.which, r, step - 1], self.place.go(axis, step))
 
     def rows_copy(self, t):
         source = self.rows.at[t.layer, 1 - self.place.at["c"]]
@@ -532,7 +539,7 @@
             total = self.spot[t.slot, r, self.place.index(axis)].astype(F32)
             for step in (1, 2, 3):
                 self.spot_copy(t, r, step).wait_recv()
-                total = total + self.spot_in[t.number, r, step - 1].astype(F32)
+                total = total + self.spot_in[t.which, r, step - 1].astype(F32)
             if not t.second:
                 self.first_out[t.section, 0, 0, r] = total.astype(BF16)
             elif r == 0:
@@ -588,32 +595,32 @@
         place, me = self.place, self.place.at["c"]
         for copy in self.now:
             copy.wait_recv()
+            copy.wait_send()
         if number == 0:
-            self.part[0] = self.small[self.half(me), :] + self.bufs[12]
+            self.part[...] = self.small[self.half(me), :] + self.bufs[12]
         else:
             axis = AXES[number - 1]
-            self.bufs[4 * number - 4 + place.at[axis]] = self.part[number - 1]
-            self.part[number] = (
+            self.bufs[4 * number - 4 + place.at[axis]] = self.part[...]
+            self.part[...] = (
                 (self.bufs[4 * number - 4] + self.bufs[4 * number - 3])
                 + (self.bufs[4 * number - 2] + self.bufs[4 * number - 1])
             )
         if number < 3:
             axis = AXES[number]
             self.now = [
-                self.send(self.part.at[number], self.bufs.at[4 * number + place.at[axis]], 1 + 3 * number + step - 1, place.go(axis, step))
+                self.send(self.part, self.bufs.at[4 * number + place.at[axis]], 1 + 3 * number + step - 1, place.go(axis, step))
                 for step in (1, 2, 3)
             ]
         else:
-            self.now = [self.send(self.part.at[3], self.bufs.at[13], 10, place.go("c", 1))]
+            self.now = [self.send(self.part, self.bufs.at[13], 10, place.go("c", 1))]
 
     def close(self, out):
         me = self.place.at["c"]
         for copy in self.now:
             copy.wait_recv()
-        out[self.half(me), :] = self.part[3]
+        out[self.half(me), :] = self.part[...]
         out[self.half(1 - me), :] = self.bufs[13]
-        for copy in self.copies:
-            copy.wait_send()
+        self.copies[-1].wait_send()
 
 
 class Spread:
@@ -760,7 +767,7 @@
     tokens, masked, cotangent, live, mask_token, norm_gain, norm_shift, layer_scale, w_own, w2_hbm,
     tables,
     block_out, tokens_grad, first_grad, second_out, totals,
-    w, w2, h, qkv, probs, o, a, slope, p, n, bias, table, select_f, by_x, fold_sums, du, dp, g, vec, vecs, small,
+    w, w2, h, qkv, probs, a, slope, p, n, bias, table, select_f, by_x, fold_sums, du, dp, g, vec, vecs, small,
     stage, pair, far, line, line_in, spot, spot_in, rows, rows_in, part, bufs, first_out,
     tokens_in, cotangent_in, load_sems, w2_sems, image_sems, gather_sems, sems, small_sems, share_sems, share_out_sems, pair_credit, far_credit,
 ):
@@ -817,7 +824,7 @@
     body = Body(
         valid=valid, core=place.at["c"], vecs=vecs, table=table,
         select_forward=select_f, by_x=by_x, block_out=tokens_in, small=small,
-        w=w, w2=w2, h=h, qkv=qkv, probs=probs, o=o, a=a, slope=slope, p=p, n=n, bias=bias,
+        w=w, w2=w2, h=h, qkv=qkv, probs=probs, a=a, slope=slope, p=p, n=n, bias=bias,
         sums=fold_sums, du=du, dp=dp, g=g, stage=stage, pair=pair,
     )
     reduce = Reduce(
@@ -882,13 +889,13 @@
 
         @pl.when(layer == 0)
         def _():
+            body.finish(1, a.at[0], w2[...])
             load_second(1)
 
         return 0
 
     lax.fori_loop(0, 2, forward_layer, 0)
     block_copy = pltpu.make_async_copy(tokens_in, block_out, image_sems.at[0])
-    block_copy.start()
     gather.drain()
 
     def backward_layer(turn, _):
@@ -904,6 +911,11 @@
 
         body.second_half(second, False)
 
+        @pl.when(turn == 0)
+        def _():
+            body.last_finish()
+            block_copy.start()
+
         @pl.when(again)
         def _():
             reduce.third(dense_before)
@@ -949,13 +961,14 @@
         body.pairs(layer, 1)
         reduce.merge(dense)
 
+        reduce.prepare(attention, second)
+        body.first_half(attention, False)
+        body.fold_bias(layer)
+
         @pl.when(again)
         def _():
             reduce.close(attention_before)
 
-        reduce.prepare(attention, second)
-        body.first_half(attention, False)
-        body.fold_bias(layer)
         reduce.third(second)
         body.leave(layer, 0)
         reduce.second(dense)
@@ -1006,15 +1019,15 @@
         out_specs=(hbm, hbm, hbm, vm, vm),
         scratch_shapes=[
             V((4, 4, 4, 48, FF), BF16), V((FF, D), BF16), V((4, ROWS, D), BF16), V((2, KEYS, 2304), BF16),
-            V((2, HEADS, 16 * GRID, KEYS), BF16), V((2, ROWS, D), BF16), V((2, ROWS, FF), BF16), V((2, ROWS, FF), BF16),
-            V((4, ROWS, D), BF16), V((2, ROWS, D), BF16), V((2, HEADS, ROWS, KEYS), BF16), V((2 * HEADS, 896), F32), V((384, KEYS), BF16),
+            V((2, HEADS, 16 * GRID, KEYS), BF16), V((2, ROWS, FF), BF16), V((2, ROWS, FF), BF16),
+            V((4, ROWS, D), BF16), V((3, ROWS, D), BF16), V((2, HEADS, ROWS, KEYS), BF16), V((2 * HEADS, 896), F32), V((384, KEYS), BF16),
             V((16 * GRID, ROWS), BF16),
             V((3, ROWS, 128), F32), V((ROWS, FF), BF16), V((ROWS, D), BF16), V((ROWS, D), BF16),
             V((8, D), F32), V((4, 8, D), F32), V((48, D), F32),
             V((2,) + HALF, BF16), V((2,) + HALF, BF16), V((2, 3, 6, 2, 4, 16, 384), BF16),
             V((2, 3, 4, 4, 16, 384), BF16), V((2, 3, 3, 4, 16, 384), BF16),
-            V((2, 3, 4, 16, 384), BF16), V((6, 3, 3, 16, 384), BF16),
-            V((2, 2, 24, 384), F32), V((2, 24, 384), F32), V((4, 24, D), F32), V((14, 24, D), F32),
+            V((2, 3, 4, 16, 384), BF16), V((3, 3, 3, 16, 384), BF16),
+            V((2, 2, 24, 384), F32), V((2, 24, 384), F32), V((24, D), F32), V((14, 24, D), F32),
             V((4, 1, 1, 3, 16, 384), BF16), V((1, SEQ, D), BF16), V((1, SEQ, D), BF16),
             DMA((2, 8)), DMA((8,)), DMA((2,)), DMA((2, GATHER_MESSAGES)), DMA((2, 6, 43)), DMA((2, 11)), DMA((2, 75)), DMA((48,)), REGULAR, REGULAR((3, 2)),
         ],

time: 190 us -> 188 us (0.989)
  Pallas kernels: 189 us -> 187 us
    pallas_call x1, Pallas kernels: 182 us -> 180 us  [layers(): pl.pallas_call(layers_kernel, out_shape=(jax.ShapeDtypeStruct((1, SEQ, D)...]
where the time goes in v2:
time: 188 us
  Pallas kernels  187 us (99%)
    pallas_call x1, Pallas kernels, layers(): pl.pallas_call(layers_kernel, out_shape=(jax.ShapeDtypeStruct((1, SEQ, D)...  180 us
    pallas_call x1, Pallas kernels, finish_all(): pl.pallas_call(finish_kernel, out_shape=(jax.ShapeDtypeStruct(image, BF16...  6.9 us

profile of v2, /device:TPU:1, one launch (start us, length us, event | category | flops | bytes accessed | tf_op | source)
XLA Modules:
  0.0 187.9 jit_solution(15204981955928529470)
XLA Ops:
  0.6 180.2 %shard_map.186 = (bf16[1,197,768]{2,1,0:T(8,128)(2,1)}, bf16[1,197,768]{2,1,0:T(8,128)(2,1)}, bf16[4,4,48,3072]{3,2,1,0:T(8,128)(2,1)}, f32[2,24,768]{2,1,0:T(8,128)}, f32[48,768]{1,0:T(8,128)}) custom-call(bf16[1,197,768]{2,1,0:T(8,128)(2,1)} %tokens.1, s32[1,197]{1,0:T(1,128)} %masked.1, bf16[1,197,768]{2,1,0:T(8,128)(2,1)} %cotangent.1, s32[32]{0:T(128)} %live.3, ...), custom_call_target="tpu_custom_call" | custom-call | tf_op jit(solution)/shard_map/pallas_call | solution.py:1009
  180.8 6.9 %shard_map.187 = (bf16[1,197,768]{2,1,0:T(8,128)(2,1)}, bf16[1,197,768]{2,1,0:T(8,128)(2,1)}, f32[1,768,3072]{2,1,0:T(8,128)}, f32[2,24,768]{2,1,0:T(8,128)}, f3...) custom-call(bf16[4,4,48,3072]{3,2,1,0:T(8,128)(2,1)} %get-tuple-elem, ...), custom_call_target="tpu_custom_call" | custom-call | tf_op jit(solution)/shard_map/pallas_call | solution.py:1191
